TPU v7x, 32 devices: a whole 2x2x4 slice. The times are simulated.
32 devices in a mesh: az: 8 (over z, y), rg: 4 (over x, core).
Axes of the slice: x: 2, y: 2, z: 4, core: 2. Of those that a mesh axis runs over, the one named last changes fastest.
Arguments:
- echoes: bfloat16 [2, 8192, 16384], P(None, 'rg', 'az'), may hold values from -6 to 6
- replica: bfloat16 [2, 2048], replicated, may hold values from -0.125 to 0.125
- shifts: int32 [512, 8], replicated, may hold values from 0 to 16, as said below
- tap_counts: int32 [512], replicated, may hold values from 1 to 8
- interp_weights: float32 [512, 8], replicated, may hold values from -2 to 2
- fm_rates: float32 [512], replicated, may hold values from 50 to 1000
Outputs:
- focused_image: float32 [2, 8192, 16384], P(None, ('rg', 'az'))
Inputs may be any that keep to these rules, and one draw needn't show every extreme that they name: `shifts`: in some range band and Doppler block the shift is 16 while that band uses all 8 taps.
All inputs are finite; a program needn't handle non-finite values.
Results may differ from a plain program's by a relative error of at most 0.0029.
Values may be sent and summed in bfloat16 or wider, within the bound.
A program may use at most 320 MiB of HBM per device.

v0:
```python
import math

import jax
import jax.numpy as jnp
from jax import lax
from jax.sharding import PartitionSpec as P

AZ_OUTER = 128
AZ_INNER = 128
INTERP_TAPS = 8
MAX_SHIFT = 16
BAND_BINS = 16
DOPPLER_BLOCKS = 8


precise = lax.Precision.HIGHEST


def shifted(value, axis, steps):
    count = lax.axis_size(axis)
    initial, last = (max(0, -steps), min(count, count - steps))
    return lax.ppermute(value, axis, [(source, source + steps) for source in range(initial, last)])


def shifted_2(block, axis, distance):
    devices = range(lax.axis_size(axis))
    route = [((i - distance) % len(devices), i) for i in devices]
    return lax.ppermute(block, axis, route)


def angle_table(row_count, col_count, period):
    product = (
        lax.broadcasted_iota(jnp.int32, (row_count, col_count), 0)
        * lax.broadcasted_iota(jnp.int32, (row_count, col_count), 1)
        % period
    )
    theta = product.astype(jnp.float32) * (2.0 * math.pi / period)
    return (jnp.cos(theta), jnp.sin(theta))


def complex_section(form, cosine, sine, real_part, imag_part, inverse):
    cos_real = jnp.einsum(form, cosine, real_part, precision=precise)
    cos_imag = jnp.einsum(form, cosine, imag_part, precision=precise)
    sin_real = jnp.einsum(form, sine, real_part, precision=precise)
    sin_imag = jnp.einsum(form, sine, imag_part, precision=precise)
    if inverse:
        return (cos_real - sin_imag, cos_imag + sin_real)
    return (cos_real + sin_imag, cos_imag - sin_real)


def forward_transform(turned):
    row_count = turned.shape[1]
    real_part = turned[0].astype(jnp.float32).reshape(row_count, AZ_OUTER, AZ_INNER)
    imag_part = turned[1].astype(jnp.float32).reshape(row_count, AZ_OUTER, AZ_INNER)
    outer_cos, outer_sin = angle_table(AZ_OUTER, AZ_OUTER, AZ_OUTER)
    twist_cos, twist_sin = angle_table(AZ_OUTER, AZ_INNER, AZ_OUTER * AZ_INNER)
    inner_cos, inner_sin = angle_table(AZ_INNER, AZ_INNER, AZ_INNER)
    first_real, first_imag = complex_section(
        "fa,rab->rfb", outer_cos, outer_sin, real_part, imag_part, False
    )
    twisted_real = first_real * twist_cos + first_imag * twist_sin
    twisted_imag = first_imag * twist_cos - first_real * twist_sin
    spec_real, spec_imag = complex_section(
        "gb,rfb->rfg", inner_cos, inner_sin, twisted_real, twisted_imag, False
    )
    return jnp.stack([spec_real, spec_imag])


def inverse_transform(focused_real, focused_imag):
    row_count = focused_real.shape[0]
    outer_cos, outer_sin = angle_table(AZ_OUTER, AZ_OUTER, AZ_OUTER)
    twist_cos, twist_sin = angle_table(AZ_OUTER, AZ_INNER, AZ_OUTER * AZ_INNER)
    inner_cos, inner_sin = angle_table(AZ_INNER, AZ_INNER, AZ_INNER)
    first_real, first_imag = complex_section(
        "bg,rfg->rfb", inner_cos, inner_sin, focused_real, focused_imag, True
    )
    twisted_real = first_real * twist_cos - first_imag * twist_sin
    twisted_imag = first_imag * twist_cos + first_real * twist_sin
    line_real, line_imag = complex_section(
        "af,rfb->rab", outer_cos, outer_sin, twisted_real, twisted_imag, True
    )
    scale = 1.0 / (AZ_OUTER * AZ_INNER)
    return (jnp.stack([line_real, line_imag]) * scale).reshape(2, row_count, AZ_OUTER * AZ_INNER)


def compress_range(padded, replica, range_count):
    tap_total = replica.shape[1]
    line_count = padded.shape[2]
    block_rows = math.gcd(512, range_count)
    piece_count = (tap_total + 2 * block_rows - 2) // block_rows
    span_cols = piece_count * block_rows

    def banded(vector):
        cycled = jnp.concatenate([vector, jnp.zeros((span_cols + 1 - tap_total,), vector.dtype)])
        return jnp.tile(cycled, block_rows)[: block_rows * span_cols].reshape(block_rows, span_cols)

    real_rows = banded(replica[0])
    imag_rows = banded(replica[1])
    weights = jnp.stack([jnp.stack([real_rows, imag_rows]), jnp.stack([-imag_rows, real_rows])])
    weights = weights.reshape(2, 2, block_rows, piece_count, block_rows).transpose(3, 0, 1, 2, 4)
    block_count = range_count // block_rows
    needed = (block_count + piece_count - 1) * block_rows
    extended = jnp.concatenate(
        [padded, jnp.zeros((2, needed - padded.shape[1], line_count), padded.dtype)], axis=1
    )
    blocks = extended.reshape(2, block_count + piece_count - 1, block_rows, line_count)
    total = jnp.zeros((2, block_count, block_rows, line_count), jnp.float32)
    for piece_idx in range(piece_count):
        total = total + jnp.einsum(
            "cdxy,dnyl->cnxl",
            weights[piece_idx],
            blocks[:, piece_idx : piece_idx + block_count],
            preferred_element_type=jnp.float32,
        )
    return total.astype(jnp.bfloat16).reshape(2, range_count, line_count)


def corner_turn(operand):
    return lax.all_to_all(operand, "az", split_axis=1, concat_axis=2, tiled=True)


def migration_matrix(shifts, tap_counts, interp_weights, band_first, row_count, ext_count):
    bands_here = row_count // BAND_BINS
    band_shift = lax.dynamic_slice(shifts, (band_first, jnp.int32(0)), (bands_here, DOPPLER_BLOCKS))
    band_taps = lax.dynamic_slice_in_dim(tap_counts, band_first, bands_here)
    band_weight = lax.dynamic_slice(
        interp_weights, (band_first, jnp.int32(0)), (bands_here, INTERP_TAPS)
    )
    row_shift = jnp.repeat(band_shift, BAND_BINS, axis=0)
    row_taps = jnp.repeat(band_taps, BAND_BINS)
    row_weight = jnp.repeat(band_weight, BAND_BINS, axis=0)
    tap_index = lax.broadcasted_iota(jnp.int32, (row_count, INTERP_TAPS), 1)
    row_index = lax.broadcasted_iota(jnp.int32, (row_count, INTERP_TAPS), 0)
    live_weight = jnp.where(tap_index < row_taps[:, None], row_weight, 0.0)
    target = (row_index + tap_index)[None] + row_shift.T[:, :, None]
    column = lax.broadcasted_iota(jnp.int32, (1, 1, 1, ext_count), 3)
    hits = (target[..., None] == column).astype(jnp.float32)
    matrix = jnp.einsum("jt,djtm->djm", live_weight, hits, precision=precise)
    return jnp.repeat(matrix, AZ_INNER // DOPPLER_BLOCKS, axis=0)


def per_device(echoes, replica, shifts, tap_counts, interp_weights, fm_rates):
    tap_total = replica.shape[1]
    range_dev, line_count = (echoes.shape[1], echoes.shape[2])
    az_count = lax.axis_size("az")
    local_rows = range_dev // az_count
    rim_bins = MAX_SHIFT + INTERP_TAPS - 1
    az_pos = lax.axis_index("az")
    rg_pos = lax.axis_index("rg")
    rim_rows = shifted(echoes[:, : tap_total - 1, :], "rg", -1)
    padded = jnp.concatenate([echoes, rim_rows], axis=1)
    compressed = compress_range(padded, replica, range_dev)
    at_end = az_pos == az_count - 1
    spectrum = forward_transform(corner_turn(compressed))
    nearby = shifted_2(spectrum[:, :rim_bins], "az", -1)
    across = shifted(nearby, "rg", -1)
    spectrum = jnp.concatenate([spectrum, jnp.where(at_end, across, nearby)], axis=1)
    band_first = (rg_pos * range_dev + az_pos * local_rows) // BAND_BINS
    matrix = migration_matrix(
        shifts, tap_counts, interp_weights, band_first, local_rows, local_rows + rim_bins
    )
    migrated = jnp.einsum("gjm,cmfg->cjfg", matrix, spectrum, precision=precise)
    row_rate = jnp.repeat(
        lax.dynamic_slice_in_dim(fm_rates, band_first, local_rows // BAND_BINS), BAND_BINS
    )
    total_lines = AZ_OUTER * AZ_INNER
    doppler = lax.broadcasted_iota(
        jnp.int32, (AZ_OUTER, AZ_INNER), 0
    ) + AZ_OUTER * lax.broadcasted_iota(jnp.int32, (AZ_OUTER, AZ_INNER), 1)
    signed = (
        jnp.where(doppler < total_lines // 2, doppler, doppler - total_lines).astype(jnp.float32)
        / total_lines
    )
    phases = math.pi * row_rate[:, None, None] * (signed * signed)[None]
    cosine = jnp.cos(phases)
    sine = jnp.sin(phases)
    focused_real = migrated[0] * cosine + migrated[1] * sine
    focused_imag = migrated[1] * cosine - migrated[0] * sine
    return inverse_transform(focused_real, focused_imag)


def solution(mesh):
    return jax.shard_map(
        per_device,
        mesh=mesh,
        in_specs=(P(None, "rg", "az"), P(), P(), P(), P(), P()),
        out_specs=P(None, ("rg", "az"), None),
        check_vma=False,
    )
```

profile of v0, /device:TPU:26, one launch (start us, length us, event | category | flops | bytes accessed | tf_op | source)
XLA Modules:
  0.0 1769.0 jit_solution(8921978146003880933)
XLA Ops:
  0.0 31.1 %copy.201 = bf16[2,2047,2048]{2,0,1:T(2,128)(2,1)} copy(bf16[2,2047,2048]{2,1,0:T(8,128)(2,1)} %bitcast.210) | data formatting | bytes 33538048
  31.1 1.9 collective-permute-start
  33.3 5.8 tile.9
  39.1 2.3 slice.85
  41.5 3.4 stack.34
  44.9 4.7 copy.139
  49.7 5.8 tile.21
  55.6 3.1 slice.86
  58.7 6.5 stack.35
  65.2 3.9 fusion.141
  69.1 4.7 maximum_bitcast_fusion
  73.8 140.3 %collective-permute-done = bf16[2,2047,2048]{2,0,1:T(2,128)(2,1)} collective-permute-done((bf16[2,2047,2048]{2,0,1:T(2,128)(2,1)}, bf16[2,2047,2048]{2,0,1:T(2,128)(2,1)}, u32[]{:S(2)}, u32[]{:S(2)}) %collective-permute-start) | collective-permute-done | bytes 16769056 | tf_op jit(solution)/shard_map/ppermute | solution.py:22
  214.1 15.4 copy.137
  229.5 138.3 %concatenate.16 = bf16[2,4096,2048]{2,1,0:T(8,128)(2,1)} concatenate(bf16[2,2048,2048]{2,1,0:T(8,128)(2,1)} %param.6, bf16[2,2047,2048]{2,1,0:T(8,128)(2,1)} %copy.137, bf16[2,1,2048]{2,1,0:T(2,128)(2,1)S(1)} %broadcast_in_dim.16), dimensions={1} | concatenate | bytes 67108864 | tf_op jit(solution)/shard_map/concatenate | solution.py:103
  367.8 54.7 %fusion.142 = (bf16[2,4,512,2048]{3,2,1,0:T(8,128)(2,1)}, bf16[2,4,512,2048]{3,2,1,0:T(8,128)(2,1)}, bf16[2,4,512,2048]{3,2,1,0:T(8,128)(2,1)}, bf16[2,4,512,2048]{3,2,1,0:T(8,128)(2,1)}, bf16[2,4,512,2048]{3,2,1,0:T(8,128)(2,1)}) fusion(bf16[2,8,512,2048]{3,2,1,0:T(8,128)(2,1)} %bitcast.208), kind=kLoop, calls=%fused_computation.179 | loop fusion | bytes 167772160 | tf_op jit(solution)/shard_map/slice | solution.py:112
  422.5 27.4 %fusion.8 = f32[4,2048,2,512,1]{1,3,4,2,0:T(8,128)} fusion(bf16[2,4,512,2048]{3,2,1,0:T(8,128)(2,1)} %get-tuple-element.12, bf16[5,2,2,512,512]{4,3,2,1,0:T(8,128)(2,1)} %maximum_bitcast_fusion), kind=kOutput, calls=%fused_computation.22 | convolution fusion | flops 17179869184 | bytes 52428800 | tf_op jit(solution)/shard_map/cdxy,dnyl->cnxl/dot_general | solution.py:109
  449.9 27.3 %fusion.9 = f32[4,2048,2,512,1]{1,3,4,2,0:T(8,128)} fusion(bf16[2,4,512,2048]{3,2,1,0:T(8,128)(2,1)} %get-tuple-element.13, bf16[5,2,2,512,512]{4,3,2,1,0:T(8,128)(2,1)} %maximum_bitcast_fusion), kind=kOutput, calls=%fused_computation.24 | convolution fusion | flops 17179869184 | bytes 52428800 | tf_op jit(solution)/shard_map/cdxy,dnyl->cnxl/dot_general | solution.py:109
  477.2 27.6 %fusion.10 = f32[4,2048,2,512,1]{1,3,4,2,0:T(8,128)} fusion(bf16[2,4,512,2048]{3,2,1,0:T(8,128)(2,1)} %get-tuple-element.14, bf16[5,2,2,512,512]{4,3,2,1,0:T(8,128)(2,1)} %maximum_bitcast_fusion), kind=kOutput, calls=%fused_computation.26 | convolution fusion | flops 17179869184 | bytes 52428800 | tf_op jit(solution)/shard_map/cdxy,dnyl->cnxl/dot_general | solution.py:109
  504.8 35.2 %fusion.11 = f32[4,2048,2,512,1]{1,3,4,2,0:T(8,128)} fusion(bf16[2,4,512,2048]{3,2,1,0:T(8,128)(2,1)S(1)} %bitcast.218, bf16[5,2,2,512,512]{4,3,2,1,0:T(8,128)(2,1)} %maximum_bitcast_fusion), kind=kOutput, calls=%fused_computation.28 | convolution fusion | flops 17179869184 | bytes 52428800 | tf_op jit(solution)/shard_map/cdxy,dnyl->cnxl/dot_general | solution.py:109
  540.0 57.1 %fusion.14 = bf16[2,4,512,2048]{3,2,0,1:T(8,128)(2,1)} fusion(bf16[2,4,512,2048]{3,2,1,0:T(8,128)(2,1)} %get-tuple-element.15, f32[4,2048,2,512,1]{1,3,4,2,0:T(8,128)} %fusion.8, f32[4,2048,2,512,1]{1,3,4,2,0:T(8,128)} %fusion.9, f32[4,2048,2,512,1]{1,3,4,2,0:T(8,128)} %fusion.10, f32[4,2048,2,512,1]{1,3,4,2,0:T(8,128)} %fusion.11, ...), kind=kOutput, calls=%fused_computation.42 | convolution fusion | flops 17221812224 | bytes 169869312 | tf_op jit(solution)/shard_map/cdxy,dnyl->cnxl/dot_general | solution.py:109
  597.0 8.5 copy.147
  605.5 48.9 %copy.148 = bf16[2,2048,2048]{2,0,1:T(2,128)(2,1)} copy(bf16[2,2048,2048]{2,1,0:T(8,128)(2,1)S(1)} %bitcast.212) | data formatting | bytes 33554432 | tf_op jit(solution)/shard_map/reshape | solution.py:115
  654.4 6.1 all-to-all-start
  661.2 226.8 %all-to-all-done = bf16[2,2048,2048]{2,0,1:T(2,128)(2,1)} async-done(((bf16[2,2048,2048]{2,0,1:T(2,128)(2,1)}), bf16[2,2048,2048]{2,0,1:T(2,128)(2,1)}, u32[]{:S(2)}, u32[]{:S(2)}) %all-to-all-start) | async-done | bytes 16777248 | tf_op jit(solution)/shard_map/all_to_all | solution.py:119
  888.0 12.2 copy.149
  900.2 6.4 fusion.143
  906.6 11.4 copy.152
  918.0 13.5 copy.153
  931.4 13.3 fusion.46
  944.7 11.4 copy.150
  956.1 13.5 copy.151
  969.6 13.2 fusion.48
  982.8 15.7 convolution_subtract_fusion.1
  998.5 15.4 convolution_add_fusion.1
  1013.9 34.0 %fusion.17 = f32[256,128,128]{2,1,0:T(8,128)} fusion(f32[256,128,128]{2,1,0:T(8,128)} %convolution_subtract_fusion.1, f32[256,128,128]{2,1,0:T(8,128)} %convolution_add_fusion.1, f32[128,128]{0,1:T(8,128)S(1)} %copy.157, f32[128,128]{0,1:T(8,128)S(1)} %copy.154), kind=kOutput, calls=%fused_computation.50 | convolution fusion | flops 6455263232 | bytes 50462720 | tf_op jit(solution)/shard_map/gb,rfb->rfg/dot_general | solution.py:43
  1047.9 33.0 %fusion.21 = f32[256,128,128]{2,1,0:T(8,128)} fusion(f32[256,128,128]{2,1,0:T(8,128)S(1)} %copy-done.2, f32[256,128,128]{2,1,0:T(8,128)} %convolution_add_fusion.1, f32[128,128]{0,1:T(8,128)S(1)} %copy.157, f32[128,128]{0,1:T(8,128)S(1)} %copy.154), kind=kOutput, calls=%fused_computation.51 | convolution fusion | flops 6455263232 | bytes 50462720 | tf_op jit(solution)/shard_map/gb,rfb->rfg/dot_general | solution.py:42
  1080.9 34.3 %subtract_bitcast_fusion.1 = f32[1,256,128,128]{3,2,1,0:T(8,128)} fusion(f32[256,128,128]{2,1,0:T(8,128)} %fusion.17, f32[256,128,128]{2,1,0:T(8,128)S(1)} %copy-done.2, f32[256,128,128]{2,1,0:T(8,128)} %convolution_add_fusion.1, f32[128,128]{0,1:T(8,128)S(1)} %copy.157, f32[128,128]{0,1:T(8,128)S(1)} %copy.154), kind=kOutput, calls=%fused_computation.39 | convolution fusion | flops 6459457536 | bytes 67239936 | tf_op jit(solution)/shard_map/gb,rfb->rfg/dot_general | solution.py:44
  1115.2 33.8 %add_bitcast_fusion.1 = f32[1,256,128,128]{3,2,1,0:T(8,128)} fusion(f32[256,128,128]{2,1,0:T(8,128)} %fusion.21, f32[256,128,128]{2,1,0:T(8,128)S(1)} %copy-done.2, f32[256,128,128]{2,1,0:T(8,128)} %convolution_add_fusion.1, f32[128,128]{0,1:T(8,128)S(1)} %copy.157, f32[128,128]{0,1:T(8,128)S(1)} %copy.154), kind=kOutput, calls=%fused_computation.40 | convolution fusion | flops 6459457536 | bytes 67239936 | tf_op jit(solution)/shard_map/gb,rfb->rfg/dot_general | solution.py:45
  1149.0 2.0 pad_maximum_fusion.1
  1151.1 35.9 %collective-permute-done.1 = f32[2,23,128,128]{3,2,1,0:T(8,128)S(1)} collective-permute-done((f32[2,23,128,128]{3,2,1,0:T(8,128)S(1)}, f32[2,23,128,128]{3,2,1,0:T(8,128)S(1)}, u32[]{:S(2)}, u32[]{:S(2)}) %collective-permute-start.1) | collective-permute-done | bytes 3014688 | tf_op jit(solution)/shard_map/ppermute | solution.py:28
  1186.9 2.1 collective-permute-start.2
  1190.3 0.8 constant_dynamic-slice_fusion.1
  1192.3 7.8 select_reduce_fusion
  1200.1 22.1 %collective-permute-done.2 = f32[2,23,128,128]{3,2,1,0:T(8,128)} collective-permute-done((f32[2,23,128,128]{3,2,1,0:T(8,128)S(1)}, f32[2,23,128,128]{3,2,1,0:T(8,128)}, u32[]{:S(2)}, u32[]{:S(2)}) %collective-permute-start.2) | collective-permute-done | bytes 3014688 | tf_op jit(solution)/shard_map/ppermute | solution.py:22
  1222.2 2.4 broadcast_select_fusion
  1224.7 24.1 %pad_maximum_fusion = f32[2,279,128,128]{3,2,1,0:T(8,128)} fusion(f32[2,23,128,128]{3,2,1,0:T(8,128)S(1)} %broadcast_select_fusion, f32[1,256,128,128]{3,2,1,0:T(8,128)} %subtract_bitcast_fusion.1, f32[1,256,128,128]{3,2,1,0:T(8,128)} %add_bitcast_fusion.1), kind=kLoop, calls=%fused_computation | loop fusion | flops 18284544 | bytes 73138176 | tf_op jit(solution)/shard_map/concatenate | solution.py:157
  1248.7 36.8 %copy.163 = f32[2,279,128,128]{2,1,0,3:T(8,128)} copy(f32[2,279,128,128]{3,2,1,0:T(8,128)} %pad_maximum_fusion) | data formatting | bytes 73138176 | tf_op jit(solution)/shard_map/concatenate | solution.py:157
  1285.5 12.4 broadcast_in_dim.39
  1297.9 92.2 %convolution_bitcast_fusion = f32[2,256,128,128]{1,2,0,3:T(8,128)} fusion(f32[2,279,128,128]{2,1,0,3:T(8,128)} %copy.163, f32[128,256,279,1]{1,2,3,0:T(8,128)} %bitcast.209), kind=kOutput, calls=%fused_computation.41 | convolution fusion | flops 28085059584 | bytes 106692608 | tf_op jit(solution)/shard_map/gjm,cmfg->cjfg/dot_general | solution.py:162
  1390.1 67.3 %fusion.7 = (f32[256,128,128]{0,1,2:T(8,128)}, f32[256,128,128]{0,1,2:T(8,128)}) fusion(f32[2,256,128,128]{1,2,0,3:T(8,128)} %convolution_bitcast_fusion, f32[128,128]{0,1:T(8,128)S(1)} %fusion.29, f32[256]{0:T(256)S(1)} %mul.266), kind=kLoop, calls=%fused_computation.17 | loop fusion | flops 29360128 | bytes 67175424 | tf_op jit(solution)/shard_map/sub | solution.py:178
  1457.4 18.2 %copy.165 = f32[256,128,128]{2,1,0:T(8,128)} copy(f32[256,128,128]{0,1,2:T(8,128)} %get-tuple-element.10) | data formatting | bytes 33554432 | tf_op jit(solution)/shard_map/add | solution.py:177
  1475.6 22.8 %fusion.42 = f32[256,128,128]{1,2,0:T(8,128)} fusion(f32[256,128,128]{2,1,0:T(8,128)} %copy.165), kind=kOutput, calls=%fused_computation.86 | convolution fusion | flops 6442680320 | bytes 33554432 | tf_op jit(solution)/shard_map/bg,rfg->rfb/dot_general | solution.py:42
  1498.4 18.3 %copy.166 = f32[256,128,128]{2,1,0:T(8,128)} copy(f32[256,128,128]{0,1,2:T(8,128)} %get-tuple-element.9) | data formatting | bytes 33554432 | tf_op jit(solution)/shard_map/sub | solution.py:178
  1516.7 22.8 %fusion.40 = f32[256,128,128]{1,2,0:T(8,128)} fusion(f32[256,128,128]{2,1,0:T(8,128)} %copy.166), kind=kOutput, calls=%fused_computation.84 | convolution fusion | flops 6442680320 | bytes 33554432 | tf_op jit(solution)/shard_map/bg,rfg->rfb/dot_general | solution.py:43
  1539.4 24.1 %convolution_subtract_fusion = f32[256,128,128]{1,2,0:T(8,128)} fusion(f32[256,128,128]{1,2,0:T(8,128)} %fusion.42, f32[256,128,128]{2,1,0:T(8,128)} %copy.166), kind=kOutput, calls=%fused_computation.45 | convolution fusion | flops 6446874624 | bytes 50331648 | tf_op jit(solution)/shard_map/bg,rfg->rfb/dot_general | solution.py:45
  1563.5 23.8 %convolution_add_fusion = f32[256,128,128]{1,2,0:T(8,128)} fusion(f32[256,128,128]{1,2,0:T(8,128)} %fusion.40, f32[256,128,128]{2,1,0:T(8,128)} %copy.165), kind=kOutput, calls=%fused_computation.44 | convolution fusion | flops 6446874624 | bytes 50331648 | tf_op jit(solution)/shard_map/bg,rfg->rfb/dot_general | solution.py:44
  1587.3 24.5 %fusion.16 = f32[256,128,128]{2,1,0:T(8,128)} fusion(f32[256,128,128]{1,2,0:T(8,128)} %convolution_subtract_fusion, f32[256,128,128]{1,2,0:T(8,128)} %convolution_add_fusion, f32[128,128]{0,1:T(8,128)S(1)} %copy-done.4, f32[128,128]{0,1:T(8,128)S(1)} %copy-done.6), kind=kOutput, calls=%fused_computation.49 | convolution fusion | flops 6455263232 | bytes 50462720 | tf_op jit(solution)/shard_map/af,rfb->rab/dot_general | solution.py:43
  1611.8 19.5 %fusion.15 = f32[256,128,128]{2,1,0:T(8,128)} fusion(f32[256,128,128]{1,2,0:T(8,128)} %convolution_add_fusion, f32[256,128,128]{1,2,0:T(8,128)S(1)} %copy-done.1, f32[128,128]{0,1:T(8,128)S(1)} %copy-done.4, f32[128,128]{0,1:T(8,128)S(1)} %copy-done.6), kind=kOutput, calls=%fused_computation.48 | convolution fusion | flops 6455263232 | bytes 50462720 | tf_op jit(solution)/shard_map/af,rfb->rab/dot_general | solution.py:42
  1631.2 22.4 %add_bitcast_fusion = f32[256,128,128]{1,2,0:T(8,128)} fusion(f32[256,128,128]{2,1,0:T(8,128)} %fusion.16, f32[256,128,128]{1,2,0:T(8,128)} %convolution_add_fusion, f32[256,128,128]{1,2,0:T(8,128)S(1)} %copy-done.1, f32[128,128]{0,1:T(8,128)S(1)} %copy-done.4, f32[128,128]{0,1:T(8,128)S(1)} %copy-done.6), kind=kOutput, calls=%fused_computation.35 | convolution fusion | flops 6459457536 | bytes 67239936 | tf_op jit(solution)/shard_map/af,rfb->rab/dot_general | solution.py:44
  1653.6 18.0 %copy.174 = f32[256,128,128]{0,2,1:T(8,128)} copy(f32[256,128,128]{1,2,0:T(8,128)} %add_bitcast_fusion) | data formatting | bytes 33554432 | tf_op jit(solution)/shard_map/add | solution.py:47
  1671.6 25.8 %subtract_bitcast_fusion = f32[256,128,128]{1,2,0:T(8,128)} fusion(f32[256,128,128]{2,1,0:T(8,128)} %fusion.15, f32[256,128,128]{1,2,0:T(8,128)} %convolution_subtract_fusion, f32[256,128,128]{1,2,0:T(8,128)} %convolution_add_fusion, f32[128,128]{0,1:T(8,128)S(1)} %copy-done.4, f32[128,128]{0,1:T(8,128)S(1)} %copy-done.6), kind=kOutput, calls=%fused_computation.36 | convolution fusion | flops 6459457536 | bytes 67239936 | tf_op jit(solution)/shard_map/af,rfb->rab/dot_general | solution.py:45
  1697.4 17.8 %copy.173 = f32[256,128,128]{0,2,1:T(8,128)} copy(f32[256,128,128]{1,2,0:T(8,128)} %subtract_bitcast_fusion) | data formatting | bytes 33554432 | tf_op jit(solution)/shard_map/sub | solution.py:47
  1715.2 22.5 %maximum_multiply_fusion = f32[2,256,16384]{1,2,0:T(8,128)} fusion(f32[1,256,16384]{1,2,0:T(8,128)} %bitcast.213, f32[1,256,16384]{1,2,0:T(8,128)} %bitcast.214), kind=kLoop, calls=%fused_computation.1 | loop fusion | flops 16777216 | bytes 67108864 | tf_op jit(solution)/shard_map/mul | solution.py:83
  1737.7 31.1 %copy.175 = f32[2,256,16384]{2,1,0:T(8,128)} copy(f32[2,256,16384]{1,2,0:T(8,128)} %maximum_multiply_fusion) | data formatting | bytes 67108864 | tf_op jit(solution)/shard_map/mul | solution.py:83
  (58 shorter events, 3.7 us)
Async XLA Ops:
  0.0 1189.1 %copy-start = (f32[512,8]{0,1:T(8,128)S(1)}, f32[512,8]{0,1:T(8,128)}, u32[]{:S(2)}) copy-start(f32[512,8]{0,1:T(8,128)} %param.10) | copy-start | bytes 49156
  0.0 33.0 %copy-start.10 = (bf16[2,2048]{1,0:T(2,128)(2,1)S(1)}, bf16[2,2048]{1,0:T(2,128)(2,1)}, u32[]{:S(2)}) copy-start(bf16[2,2048]{1,0:T(2,128)(2,1)} %param.7) | copy-start | bytes 24580
  31.1 183.0 %collective-permute-start = (bf16[2,2047,2048]{2,0,1:T(2,128)(2,1)}, bf16[2,2047,2048]{2,0,1:T(2,128)(2,1)}, u32[]{:S(2)}, u32[]{:S(2)}) collective-permute-start(bf16[2,2047,2048]{2,0,1:T(2,128)(2,1)} %copy.201), channel_id=1, source_target_pairs={{1,0},{2,1},{3,2},{5,4},{6,5},{7,6},{9,8},{10,9},{11,10},{13,12},{... | collective-permute-start | bytes 50307080 | tf_op jit(solution)/shard_map/ppermute | solution.py:22
  55.6 13.5 copy-start.7
  449.9 54.9 %slice-start = ((s8[16777216]{0:T(1024)(128)(4,1)}), s8[4194304]{0:T(1024)(128)(4,1)S(1)}, s32[]{:S(2)}) async-start(s8[16777216]{0:T(1024)(128)(4,1)} %bitcast.217), calls=%async_computation.1 | async-start | bytes 8388608
  449.9 54.9 %slice-start.1 = ((s8[16777216]{0:T(1024)(128)(4,1)}), s8[4194304]{0:T(1024)(128)(4,1)S(1)}, s32[]{:S(2)}) async-start(s8[16777216]{0:T(1024)(128)(4,1)} %bitcast.217), calls=%async_computation.2 | async-start | bytes 8388608
  477.2 27.6 %slice-start.2 = ((s8[16777216]{0:T(1024)(128)(4,1)}), s8[4194304]{0:T(1024)(128)(4,1)S(1)}, s32[]{:S(2)}) async-start(s8[16777216]{0:T(1024)(128)(4,1)} %bitcast.217), calls=%async_computation.3 | async-start | bytes 8388608
  477.2 27.6 %slice-start.3 = ((s8[16777216]{0:T(1024)(128)(4,1)}), s8[4194304]{0:T(1024)(128)(4,1)S(1)}, s32[]{:S(2)}) async-start(s8[16777216]{0:T(1024)(128)(4,1)} %bitcast.217), calls=%async_computation.4 | async-start | bytes 8388608
  654.4 233.6 %all-to-all-start = ((bf16[2,2048,2048]{2,0,1:T(2,128)(2,1)}), bf16[2,2048,2048]{2,0,1:T(2,128)(2,1)}, u32[]{:S(2)}, u32[]{:S(2)}) async-start(bf16[2,2048,2048]{2,0,1:T(2,128)(2,1)} %copy.148), calls=%async_computation | async-start | bytes 33554432 | tf_op jit(solution)/shard_map/all_to_all | solution.py:119
  660.8 454.4 %copy-start.3 = (f32[128,128]{0,1:T(8,128)}, f32[128,128]{0,1:T(8,128)S(1)}, u32[]{:S(2)}) copy-start(f32[128,128]{0,1:T(8,128)S(1)} %copy.157) | copy-start | bytes 196612
  661.2 454.0 %copy-start.5 = (f32[128,128]{0,1:T(8,128)}, f32[128,128]{0,1:T(8,128)S(1)}, u32[]{:S(2)}) copy-start(f32[128,128]{0,1:T(8,128)S(1)} %copy.154) | copy-start | bytes 196612
  1013.9 34.1 %copy-start.2 = (f32[256,128,128]{2,1,0:T(8,128)S(1)}, f32[256,128,128]{2,1,0:T(8,128)}, u32[]{:S(2)}) copy-start(f32[256,128,128]{2,1,0:T(8,128)} %convolution_subtract_fusion.1) | copy-start | bytes 50331652
  1151.0 35.9 %collective-permute-start.1 = (f32[2,23,128,128]{3,2,1,0:T(8,128)S(1)}, f32[2,23,128,128]{3,2,1,0:T(8,128)S(1)}, u32[]{:S(2)}, u32[]{:S(2)}) collective-permute-start(f32[2,23,128,128]{3,2,1,0:T(8,128)S(1)} %pad_maximum_fusion.1), channel_id=1, source_target_pairs={{4,0},{8,4},{12,8},{16,12},{20,16},{24,20},{28,24},{0,28},{5,1},{9... | collective-permute-start | bytes 9043976 | tf_op jit(solution)/shard_map/ppermute | solution.py:28
  1186.9 13.2 copy-start.9
  1186.9 35.3 %collective-permute-start.2 = (f32[2,23,128,128]{3,2,1,0:T(8,128)S(1)}, f32[2,23,128,128]{3,2,1,0:T(8,128)}, u32[]{:S(2)}, u32[]{:S(2)}) collective-permute-start(f32[2,23,128,128]{3,2,1,0:T(8,128)S(1)} %collective-permute-done.1), channel_id=1, source_target_pairs={{1,0},{2,1},{3,2},{5,4},{6,5},{7,6},{9,8},{10,9},{11,10},{13,12},{... | collective-permute-start | bytes 9043976 | tf_op jit(solution)/shard_map/ppermute | solution.py:22
  1248.7 36.8 %copy-start.8 = (f32[256,8,279]{0,2,1:T(8,128)S(1)}, f32[256,8,279]{0,2,1:T(8,128)}, u32[]{:S(2)}) copy-start(f32[256,8,279]{0,2,1:T(8,128)} %select_reduce_fusion) | copy-start | bytes 6856708
  1563.5 23.8 %copy-start.4 = (f32[128,128]{0,1:T(8,128)S(1)}, f32[128,128]{0,1:T(8,128)}, u32[]{:S(2)}) copy-start(f32[128,128]{0,1:T(8,128)} %copy-done.3) | copy-start | bytes 196612
  1563.5 23.8 %copy-start.6 = (f32[128,128]{0,1:T(8,128)S(1)}, f32[128,128]{0,1:T(8,128)}, u32[]{:S(2)}) copy-start(f32[128,128]{0,1:T(8,128)} %copy-done.5) | copy-start | bytes 196612
  1587.3 24.5 %copy-start.1 = (f32[256,128,128]{1,2,0:T(8,128)S(1)}, f32[256,128,128]{1,2,0:T(8,128)}, u32[]{:S(2)}) copy-start(f32[256,128,128]{1,2,0:T(8,128)} %convolution_subtract_fusion) | copy-start | bytes 50331652
where the time goes:
time: 1790 us; the launch traced here: 1770 us
  matrix products  645 us (36%)
  local copies, waits for them, and re-layouts  552 us (31%)
  waiting for transfers between devices  425 us (24%)
  other arithmetic  136 us (8%)
    all_to_all x1, waiting for transfers between devices, corner_turn(): lax.all_to_all(operand, 'az', split_axis=1, concat_axis=2, tiled=True)  227 us
    dot_general x5, matrix products, compress_range(): jnp.einsum('cdxy,dnyl->cnxl', weights[piece_idx], blocks[:, piece_idx:pie...  174 us
    ppermute x2, waiting for transfers between devices, shifted(): lax.ppermute(value, axis, [(source, source + steps) for source in range(i...  162 us
    concatenate x1, local copies, waits for them, and re-layouts, compress_range(): jnp.concatenate([padded, jnp.zeros((2, needed - padded.shape[1], line_cou...  138 us
    dot_general x4, matrix products, complex_section(): sin_imag = jnp.einsum(form, sine, imag_part, precision=precise)  99.1 us
    dot_general x4, matrix products, complex_section(): sin_real = jnp.einsum(form, sine, real_part, precision=precise)  96.1 us
    dot_general x4, matrix products, complex_section(): cos_imag = jnp.einsum(form, cosine, imag_part, precision=precise)  94.6 us
    dot_general x1, matrix products, per_device(): migrated = jnp.einsum('gjm,cmfg->cjfg', matrix, spectrum, precision=precise)  92.2 us
  transfers between devices with their start and end apart: 4, of which 4 were waited for; matrix products, arithmetic and copies ran while one was open for 3% of the time, Pallas kernels for 0%

commit v1 on v0

v1 whole, which is shorter than its diff:
```python
import functools
import math

import jax
import jax.numpy as jnp
import numpy as np
from jax import lax
from jax.experimental import pallas as pl
from jax.experimental.pallas import tpu as pltpu
from jax.sharding import PartitionSpec as P

SIDE = 128
INTERP_TAPS = 8
MAX_SHIFT = 16
BAND_BINS = 16
DOPPLER_BLOCKS = 8
CHUNKS = 2
RIM_ROWS = 32
VMEM = 56 * 1024 * 1024


def transform_tables():
    k = np.arange(SIDE)
    angle = 2.0 * np.pi * ((k[:, None] * k[None, :]) % SIDE) / SIDE
    c, s = np.cos(angle), np.sin(angle)
    forward = np.block([[c, s], [-s, c]])
    inverse = np.block([[c, -s], [s, c]])
    twist = 2.0 * np.pi * (k[:, None] * k[None, :]) / (SIDE * SIDE)
    return forward, inverse, np.cos(twist), np.sin(twist)


def split_const(matrix):
    high = jnp.asarray(matrix, jnp.float32).astype(jnp.bfloat16)
    low_np = np.asarray(matrix, np.float64) - np.asarray(
        np.asarray(matrix, np.float32).astype(jnp.bfloat16), np.float64
    )
    return jnp.stack([high, jnp.asarray(low_np, jnp.float32).astype(jnp.bfloat16)])


def split_data(value):
    high = value.astype(jnp.bfloat16)
    return high, (value - high.astype(jnp.float32)).astype(jnp.bfloat16)


NN = (((1,), (0,)), ((), ()))
NT = (((1,), (1,)), ((), ()))


def mm(a, b, dims):
    return lax.dot_general(a, b, dims, preferred_element_type=jnp.float32)


def mm2(table, data, dims):
    return mm(table[0], data, dims) + mm(table[1], data, dims)


def mm3(table, value, dims):
    high, low = split_data(value)
    return mm(table[0], high, dims) + (mm(table[1], high, dims) + mm(table[0], low, dims))


def compress_kernel(chunk, block_rows, local_rows, w_ref, own_ref, rim_ref, out_ref, window):
    dest = pl.program_id(1)
    own_rows = own_ref.shape[1]

    @pl.when(dest == 0)
    def _():
        window[:, :own_rows, :] = own_ref[...]
        window[:, own_rows:, :] = rim_ref[...]

    start = pl.multiple_of(dest * local_rows + chunk * block_rows, block_rows)
    span = w_ref.shape[2]
    total = mm(w_ref[0], window[0, pl.ds(start, span), :], NN)
    total = total + mm(w_ref[1], window[1, pl.ds(start, span), :], NN)
    total = total.astype(jnp.bfloat16)
    out_ref[0, 0] = total[:block_rows]
    out_ref[0, 1] = total[block_rows:]


def compress(weights, echoes, rim, chunk, az_count, local_rows):
    range_dev, lines = echoes.shape[1], echoes.shape[2]
    taps = rim.shape[1]
    block_rows = local_rows // CHUNKS
    tile = math.gcd(512, lines)
    span = weights.shape[2]
    return pl.pallas_call(
        functools.partial(compress_kernel, chunk, block_rows, local_rows),
        out_shape=jax.ShapeDtypeStruct((az_count, 2, block_rows, lines), jnp.bfloat16),
        grid=(lines // tile, az_count),
        in_specs=[
            pl.BlockSpec(weights.shape, lambda l, j: (0, 0, 0)),
            pl.BlockSpec((2, range_dev, tile), lambda l, j: (0, 0, l)),
            pl.BlockSpec((2, taps, tile), lambda l, j: (0, 0, l)),
        ],
        out_specs=pl.BlockSpec((1, 2, block_rows, tile), lambda l, j: (j, 0, 0, l)),
        scratch_shapes=[pltpu.VMEM((2, range_dev + taps, tile), jnp.bfloat16)],
        compiler_params=pltpu.CompilerParams(vmem_limit_bytes=VMEM),
        cost_estimate=pl.CostEstimate(
            flops=8 * az_count * block_rows * span * lines,
            bytes_accessed=4 * lines * (2 * range_dev + taps),
            transcendentals=0,
        ),
        name=f"compress_{chunk}",
    )(weights, echoes, rim)


def compress_weights(replica, block_rows):
    taps = replica.shape[1]
    span = taps + block_rows

    def banded(vector):
        cycled = jnp.concatenate([vector, jnp.zeros((span + 1 - taps,), vector.dtype)])
        return jnp.tile(cycled, block_rows)[: block_rows * span].reshape(block_rows, span)

    real_rows = banded(replica[0])
    imag_rows = banded(replica[1])
    return jnp.stack(
        [
            jnp.concatenate([real_rows, -imag_rows], axis=0),
            jnp.concatenate([imag_rows, real_rows], axis=0),
        ]
    )


def forward_kernel(table_ref, cos_ref, sin_ref, in_ref, *rest):
    out_ref, data = rest[-2], rest[-1]
    az_count, _, rows, lines = in_ref.shape
    per = lines // SIDE
    for source in range(az_count):
        for c in range(2):
            piece = in_ref[source, c].astype(jnp.float32)
            data[:, c * SIDE + source * per : c * SIDE + (source + 1) * per, :] = piece.reshape(
                rows, per, SIDE
            )

    def pair(i, _):
        both = jnp.concatenate([data[2 * i], data[2 * i + 1]], axis=1).astype(jnp.bfloat16)
        first = mm2(table_ref, both, NN)
        cosine, sine = cos_ref[...], sin_ref[...]
        turned = []
        for k in range(2):
            real = first[:SIDE, k * SIDE : (k + 1) * SIDE]
            imag = first[SIDE:, k * SIDE : (k + 1) * SIDE]
            turned.append(
                jnp.concatenate(
                    [real * cosine + imag * sine, imag * cosine - real * sine], axis=1
                )
            )
        second = mm3(table_ref, jnp.concatenate(turned, axis=0), NT)
        for k in range(2):
            out_ref[0, 2 * i + k] = second[:SIDE, k * SIDE : (k + 1) * SIDE]
            out_ref[1, 2 * i + k] = second[SIDE:, k * SIDE : (k + 1) * SIDE]
        return 0

    lax.fori_loop(0, rows // 2, pair, 0, unroll=2)


def forward(tables, lines_in, held, first_block, total_rows):
    table, cosine, sine = tables
    az_count, _, rows, lines = lines_in.shape
    whole2 = lambda i: (0, 0)
    in_specs = [
        pl.BlockSpec(table.shape, lambda i: (0, 0, 0)),
        pl.BlockSpec((SIDE, SIDE), whole2),
        pl.BlockSpec((SIDE, SIDE), whole2),
        pl.BlockSpec((az_count, 2, BAND_BINS, lines), lambda i: (0, 0, i, 0)),
    ]
    operands = [table, cosine, sine, lines_in]
    aliases = {}
    if held is not None:
        in_specs.append(pl.BlockSpec(memory_space=pl.ANY))
        operands.append(held)
        aliases = {4: 0}
    return pl.pallas_call(
        forward_kernel,
        out_shape=jax.ShapeDtypeStruct((2, total_rows, SIDE, SIDE), jnp.float32),
        grid=(rows // BAND_BINS,),
        in_specs=in_specs,
        out_specs=pl.BlockSpec((2, BAND_BINS, SIDE, SIDE), lambda i: (0, first_block + i, 0, 0)),
        scratch_shapes=[pltpu.VMEM((BAND_BINS, 2 * SIDE, SIDE), jnp.float32)],
        input_output_aliases=aliases,
        compiler_params=pltpu.CompilerParams(vmem_limit_bytes=VMEM),
        cost_estimate=pl.CostEstimate(
            flops=rows * 5 * 2 * 2 * SIDE * 2 * SIDE * SIDE * 2,
            bytes_accessed=rows * SIDE * SIDE * 12,
            transcendentals=0,
        ),
        name=f"forward_at_{first_block}",
    )(*operands)


def focus_kernel(
    shift_ref, weight_ref, table_ref, cos_ref, sin_ref, pcos_ref, psin_ref,
    spec0, spec1, spec2, out_ref, window, moved, image
):
    band = pl.program_id(0)
    for k, ref in enumerate((spec0, spec1, spec2)):
        keep = BAND_BINS if k < 2 else INTERP_TAPS
        window[:, k * BAND_BINS : k * BAND_BINS + keep] = ref[:, :keep]
    deep = SIDE // DOPPLER_BLOCKS
    taps = [weight_ref[band, t] for t in range(INTERP_TAPS)]

    def block(d, _):
        shift = shift_ref[band, d]
        spot = pl.ds(pl.multiple_of(d * deep, deep), deep)
        pcos, psin = pcos_ref[0, spot, :], psin_ref[0, spot, :]
        sums = []
        for half in range(2):
            rows = BAND_BINS // 2
            parts = []
            for c in range(2):
                total = taps[0] * window[c, pl.ds(shift + half * rows, rows), spot, :]
                for t in range(1, INTERP_TAPS):
                    total = total + taps[t] * window[c, pl.ds(shift + half * rows + t, rows), spot, :]
                parts.append(total)
            real, imag = parts
            put = slice(half * rows, (half + 1) * rows)
            moved[put, spot, :] = real * pcos + imag * psin
            low = pl.ds(pl.multiple_of(SIDE + d * deep, deep), deep)
            moved[put, low, :] = imag * pcos - real * psin
        return 0

    lax.fori_loop(0, DOPPLER_BLOCKS, block, 0)

    def pair(i, _):
        both = jnp.concatenate([moved[2 * i], moved[2 * i + 1]], axis=1)
        first = mm3(table_ref, both, NN)
        cosine, sine = cos_ref[...], sin_ref[...]
        turned = []
        for k in range(2):
            real = first[:SIDE, k * SIDE : (k + 1) * SIDE]
            imag = first[SIDE:, k * SIDE : (k + 1) * SIDE]
            turned.append(
                jnp.concatenate(
                    [real * cosine - imag * sine, imag * cosine + real * sine], axis=1
                )
            )
        second = mm2(table_ref, jnp.concatenate(turned, axis=0).astype(jnp.bfloat16), NT)
        second = second * (1.0 / (SIDE * SIDE))
        for k in range(2):
            image[2 * i + k] = second[:, k * SIDE : (k + 1) * SIDE]
        return 0

    lax.fori_loop(0, BAND_BINS // 2, pair, 0, unroll=2)
    group = 16
    for c in range(2):
        for g in range(SIDE // group):
            piece = image[:, c * SIDE + g * group : c * SIDE + (g + 1) * group, :]
            out_ref[c, :, g * group * SIDE : (g + 1) * group * SIDE] = piece.reshape(
                BAND_BINS, group * SIDE
            )


def focus(shifts, weights, tables, pcos, psin, spectrum, local_rows):
    table, cosine, sine = tables
    whole2 = lambda i, *_: (0, 0)

    def part(k):
        return pl.BlockSpec((2, BAND_BINS, SIDE, SIDE), lambda i, *_: (0, i + k, 0, 0))

    phase_spec = pl.BlockSpec((1, SIDE, SIDE), lambda i, *_: (i, 0, 0))
    return pl.pallas_call(
        focus_kernel,
        out_shape=jax.ShapeDtypeStruct((2, local_rows, SIDE * SIDE), jnp.float32),
        grid_spec=pltpu.PrefetchScalarGridSpec(
            num_scalar_prefetch=2,
            grid=(local_rows // BAND_BINS,),
            in_specs=[
                pl.BlockSpec(table.shape, lambda i, *_: (0, 0, 0)),
                pl.BlockSpec((SIDE, SIDE), whole2),
                pl.BlockSpec((SIDE, SIDE), whole2),
                phase_spec,
                phase_spec,
                part(0),
                part(1),
                part(2),
            ],
            out_specs=pl.BlockSpec((2, BAND_BINS, SIDE * SIDE), lambda i, *_: (0, i, 0)),
            scratch_shapes=[
                pltpu.VMEM((2, 2 * BAND_BINS + INTERP_TAPS, SIDE, SIDE), jnp.float32),
                pltpu.VMEM((BAND_BINS, 2 * SIDE, SIDE), jnp.float32),
                pltpu.VMEM((BAND_BINS, 2 * SIDE, SIDE), jnp.float32),
            ],
        ),
        compiler_params=pltpu.CompilerParams(vmem_limit_bytes=VMEM),
        name="focus",
    )(shifts, weights, table, cosine, sine, pcos, psin, spectrum, spectrum, spectrum)


def per_device(echoes, replica, shifts, tap_counts, interp_weights, fm_rates):
    tap_total = replica.shape[1]
    range_dev = echoes.shape[1]
    az_count = lax.axis_size("az")
    rg_count = lax.axis_size("rg")
    local_rows = range_dev // az_count
    block_rows = local_rows // CHUNKS
    bands_here = local_rows // BAND_BINS
    az_pos = lax.axis_index("az")
    rg_pos = lax.axis_index("rg")

    rim = lax.ppermute(
        echoes[:, :tap_total], "rg", [(i, i - 1) for i in range(1, rg_count)]
    )
    weights = compress_weights(replica, block_rows)
    forward_m, inverse_m, twist_cos, twist_sin = transform_tables()
    cosine = jnp.asarray(twist_cos, jnp.float32)
    sine = jnp.asarray(twist_sin, jnp.float32)
    forward_tables = (split_const(forward_m), cosine, sine)
    inverse_tables = (split_const(inverse_m), cosine, sine)

    band_first = (rg_pos * range_dev + az_pos * local_rows) // BAND_BINS
    band_shift = lax.dynamic_slice_in_dim(shifts, band_first, bands_here)
    band_taps = lax.dynamic_slice_in_dim(tap_counts, band_first, bands_here)
    band_weight = lax.dynamic_slice_in_dim(interp_weights, band_first, bands_here)
    tap_index = lax.broadcasted_iota(jnp.int32, (bands_here, INTERP_TAPS), 1)
    live_weight = jnp.where(tap_index < band_taps[:, None], band_weight, 0.0)
    band_rate = lax.dynamic_slice_in_dim(fm_rates, band_first, bands_here)
    total_lines = SIDE * SIDE
    doppler = SIDE * lax.broadcasted_iota(jnp.int32, (SIDE, SIDE), 0) + lax.broadcasted_iota(
        jnp.int32, (SIDE, SIDE), 1
    )
    signed = (
        jnp.where(doppler < total_lines // 2, doppler, doppler - total_lines).astype(jnp.float32)
        / total_lines
    )
    phases = math.pi * band_rate[:, None, None] * (signed * signed)[None]
    pcos = jnp.cos(phases)
    psin = jnp.sin(phases)

    def turn(chunk):
        part = compress(weights, echoes, rim, chunk, az_count, local_rows)
        return lax.all_to_all(part, "az", split_axis=0, concat_axis=0, tiled=True)

    turned = [turn(chunk) for chunk in range(CHUNKS)]
    place = [a * rg_count + g for g in range(rg_count) for a in range(az_count)]
    beyond = lax.ppermute(
        turned[0][:, :, :RIM_ROWS], ("az", "rg"), list(zip(place[1:], place[:-1]))
    )
    total_rows = local_rows + RIM_ROWS
    step = block_rows // BAND_BINS
    spectrum = forward(forward_tables, turned[0], None, 0, total_rows)
    spectrum = forward(forward_tables, beyond, spectrum, CHUNKS * step, total_rows)
    for chunk in range(1, CHUNKS):
        spectrum = forward(forward_tables, turned[chunk], spectrum, chunk * step, total_rows)
    return focus(band_shift, live_weight, inverse_tables, pcos, psin, spectrum, local_rows)


def solution(mesh):
    return jax.shard_map(
        per_device,
        mesh=mesh,
        in_specs=(P(None, "rg", "az"), P(), P(), P(), P(), P()),
        out_specs=P(None, ("rg", "az"), None),
        check_vma=False,
    )
```

time: 1790 us -> 696 us (0.39); the launches traced: 1770 us -> 695 us
  matrix products: 645 us -> 0 us
  local copies, waits for them, and re-layouts: 552 us -> 10.5 us
  Pallas kernels: 0 us -> 319 us
  other arithmetic: 136 us -> 8.2 us
  waiting for transfers between devices: 425 us -> 316 us
  starting transfers between devices: 10.1 us -> 40.7 us
    dot_general x22 -> x0, matrix products: 645 us -> none  [the longest x5 174 us: compress_range(): jnp.einsum('cdxy,dnyl->cnxl', weights[piece_idx], blocks[:, piece_idx:pie...]
    pallas_call x0 -> x6, Pallas kernels: none -> 319 us  [the longest x2 118 us: compress(): pl.pallas_call(functools.partial(compress_kernel, chunk, block_rows, loca...]
    concatenate x4 -> x2, local copies, waits for them, and re-layouts: 175 us -> 0.01 us  [banded(): jnp.concatenate([vector, jnp.zeros((span + 1 - taps,), vector.dtype)])]
    all_to_all x1 -> x2, waiting for transfers between devices: 227 us -> 92 us  [turn(): return lax.all_to_all(part, 'az', split_axis=0, concat_axis=0, tiled=True)]
    slice x7 -> x4, local copies, waits for them, and re-layouts: 89.3 us -> 4.04 us  [the longest x1 3.14 us: per_device(): turned[0][:, :, :RIM_ROWS]]
    reshape x4 -> x2, local copies, waits for them, and re-layouts: 75.9 us -> 1.23 us  [banded(): jnp.tile(cycled, block_rows)[:block_rows * span].reshape(block_rows, span)]
    sub x1 -> x0, other arithmetic: 67.3 us -> none  [per_device(): focused_imag = migrated[1] * cosine - migrated[0] * sine]
    add x3 -> x0, local copies, waits for them, and re-layouts: 44.7 us -> none  [the longest x1 18.2 us: per_device(): focused_real = migrated[0] * cosine + migrated[1] * sine]
  transfers between devices with their start and end apart: 4 -> 4, of which waited for: 4 -> 4; matrix products, arithmetic and copies ran while one was open for 3% -> 2% of each run, Pallas kernels for 0% -> 16%
where the time goes in v1:
time: 696 us; the launch traced here: 695 us
  Pallas kernels  319 us (46%)
  waiting for transfers between devices  316 us (45%)
  starting transfers between devices  40.7 us (6%)
  local copies, waits for them, and re-layouts  10.5 us (2%)
  other arithmetic  8.2 us (1%)
    ppermute x1, waiting for transfers between devices, per_device(): lax.ppermute(echoes[:, :tap_total], 'rg', [(i, i - 1) for i in range(1, r...  176 us
    pallas_call x2, Pallas kernels, compress(): pl.pallas_call(functools.partial(compress_kernel, chunk, block_rows, loca...  118 us
    pallas_call x1, Pallas kernels, focus(): pl.pallas_call(focus_kernel, out_shape=jax.ShapeDtypeStruct((2, local_row...  112 us
    all_to_all x2, waiting for transfers between devices, turn(): return lax.all_to_all(part, 'az', split_axis=0, concat_axis=0, tiled=True)  92 us
    pallas_call x3, Pallas kernels, forward(): pl.pallas_call(forward_kernel, out_shape=jax.ShapeDtypeStruct((2, total_r...  89.5 us
    ppermute x1, waiting for transfers between devices, per_device(): lax.ppermute(turned[0][:, :, :RIM_ROWS], ('az', 'rg'), list(zip(place[1:]...  48.4 us
    all_to_all x2, starting transfers between devices, turn(): return lax.all_to_all(part, 'az', split_axis=0, concat_axis=0, tiled=True)  35.2 us
  transfers between devices with their start and end apart: 4, of which 4 were waited for; matrix products, arithmetic and copies ran while one was open for 2% of the time, Pallas kernels for 16%

profile of v1, /device:TPU:26, one launch (start us, length us, event | category | flops | bytes accessed | tf_op | source)
XLA Modules:
  0.0 694.9 jit_solution(15374065884512527461)
XLA Ops:
  0.0 0.0 copy-start
  0.0 2.0 collective-permute-start
  2.1 0.8 slice_reduce_fusion
  3.0 0.7 tile.9
  3.7 0.6 reshape.30
  4.4 0.7 tile.21
  5.2 0.6 reshape.31
  5.8 0.1 neg.3
  5.9 0.2 maximum_bitcast_fusion
  6.1 1.6 pad_maximum_fusion.w_ref
  7.7 175.5 %collective-permute-done.rim_ref = bf16[2,2048,2048]{2,1,0:T(8,128)(2,1)} collective-permute-done((bf16[2,2048,2048]{2,1,0:T(8,128)(2,1)}, bf16[2,2048,2048]{2,1,0:T(8,128)(2,1)}, u32[]{:S(2)}, u32[]{:S(2)}) %collective-permute-start) | collective-permute-done | bytes 16777248 | tf_op jit(solution)/shard_map/ppermute | solution.py:301
  183.2 59.0 %compress_0.1 = bf16[8,2,128,2048]{3,2,1,0:T(8,128)(2,1)} custom-call(bf16[2,256,2176]{2,1,0:T(8,128)(2,1)} %pad_maximum_fusion.w_ref, bf16[2,2048,2048]{2,1,0:T(8,128)(2,1)} %own_ref.3, bf16[2,2048,2048]{2,1,0:T(8,128)(2,1)} %collective-permute-done.rim_ref), custom_call_target="tpu_custom_call" | custom-call | flops 36507222016 | bytes 50331648 | tf_op jit(solution)/shard_map/compress_0/pallas_call | solution.py:86
  242.2 6.1 all-to-all-start.1
  248.3 59.0 %compress_1.1 = bf16[8,2,128,2048]{3,2,1,0:T(8,128)(2,1)} custom-call(bf16[2,256,2176]{2,1,0:T(8,128)(2,1)} %pad_maximum_fusion.w_ref, bf16[2,2048,2048]{2,1,0:T(8,128)(2,1)} %own_ref.3, bf16[2,2048,2048]{2,1,0:T(8,128)(2,1)} %collective-permute-done.rim_ref), custom_call_target="tpu_custom_call" | custom-call | flops 36507222016 | bytes 50331648 | tf_op jit(solution)/shard_map/compress_1/pallas_call | solution.py:86
  307.3 65.9 %all-to-all-done.1.in_ref = bf16[8,2,128,2048]{3,2,1,0:T(8,128)(2,1)} async-done(((bf16[8,2,128,2048]{3,2,1,0:T(8,128)(2,1)}), bf16[8,2,128,2048]{3,2,1,0:T(8,128)(2,1)}, u32[]{:S(2)}, u32[]{:S(2)}) %all-to-all-start.1) | async-done | bytes 8388640 | tf_op jit(solution)/shard_map/all_to_all | solution.py:332
  373.2 29.1 %all-to-all-start = ((bf16[8,2,128,2048]{3,2,1,0:T(8,128)(2,1)}), bf16[8,2,128,2048]{3,2,1,0:T(8,128)(2,1)}, u32[]{:S(2)}, u32[]{:S(2)}) async-start(bf16[8,2,128,2048]{3,2,1,0:T(8,128)(2,1)} %compress_1.1), calls=%async_computation | async-start | bytes 16777216 | tf_op jit(solution)/shard_map/all_to_all | solution.py:332
  402.3 0.8 dynamic_slice.13
  403.0 0.0 copy-done
  403.0 0.1 constant_dynamic-slice_fusion
  403.1 0.1 copy.20
  403.2 0.8 dynamic-slice_multiply_fusion
  403.9 0.7 fusion.3.weight_ref
  404.6 0.1 fusion.2
  404.7 4.8 multiply_sine_fusion
  409.5 3.1 slice.22
  412.6 3.5 collective-permute-start.1
  416.2 0.8 constant_dynamic-slice_fusion.1
  417.0 0.7 copy.19.shift_ref
  417.6 38.9 %forward_at_0.1.rest_0_ = f32[2,288,128,128]{3,2,1,0:T(8,128)} custom-call(bf16[2,256,256]{2,1,0:T(8,128)(2,1)} %constant.79.table_ref, f32[128,128]{1,0:T(8,128)} %constant.60.clone.cos_ref, f32[128,128]{1,0:T(8,128)} %constant.61.clone.sin_ref, bf16[8,2,128,2048]{3,2,1,0:T(8,128)(2,1)} %all-to-all-done.1.in_ref), custom_call_target="tpu_custom_call" | custom-call | flops 21474836480 | bytes 25165824 | tf_op jit(solution)/shard_map/forward_at_0/pallas_call | solution.py:174
  456.5 48.4 %collective-permute-done.1.in_ref = bf16[8,2,32,2048]{3,2,1,0:T(8,128)(2,1)S(1)} collective-permute-done((bf16[8,2,32,2048]{3,2,1,0:T(8,128)(2,1)}, bf16[8,2,32,2048]{3,2,1,0:T(8,128)(2,1)S(1)}, u32[]{:S(2)}, u32[]{:S(2)}) %collective-permute-start.1) | collective-permute-done | bytes 2097184 | tf_op jit(solution)/shard_map/ppermute | solution.py:336
  504.9 0.0 copy-start.2
  504.9 1.3 copy-done.2
  506.2 11.7 %forward_at_16.1.rest_0_ = f32[2,288,128,128]{3,2,1,0:T(8,128)} custom-call(bf16[2,256,256]{2,1,0:T(8,128)(2,1)} %constant.79.table_ref, f32[128,128]{1,0:T(8,128)} %constant.60.clone.cos_ref, f32[128,128]{1,0:T(8,128)} %constant.61.clone.sin_ref, bf16[8,2,32,2048]{3,2,1,0:T(8,128)(2,1)} %copy-done.2, ...), custom_call_target="tpu_custom_call", output_to_operand_aliasing={{}: (4, {})} | custom-call | flops 5368709120 | bytes 6291456 | tf_op jit(solution)/shard_map/forward_at_16/pallas_call | solution.py:174
  517.9 26.1 %all-to-all-done.in_ref = bf16[8,2,128,2048]{3,2,1,0:T(8,128)(2,1)} async-done(((bf16[8,2,128,2048]{3,2,1,0:T(8,128)(2,1)}), bf16[8,2,128,2048]{3,2,1,0:T(8,128)(2,1)}, u32[]{:S(2)}, u32[]{:S(2)}) %all-to-all-start) | async-done | bytes 8388640 | tf_op jit(solution)/shard_map/all_to_all | solution.py:332
  544.0 38.9 %forward_at_8.1.spec0.spec1.spec2 = f32[2,288,128,128]{3,2,1,0:T(8,128)} custom-call(bf16[2,256,256]{2,1,0:T(8,128)(2,1)} %constant.79.table_ref, f32[128,128]{1,0:T(8,128)} %constant.60.clone.cos_ref, f32[128,128]{1,0:T(8,128)} %constant.61.clone.sin_ref, bf16[8,2,128,2048]{3,2,1,0:T(8,128)(2,1)} %all-to-all-done.in_ref, ...), custom_call_target="tpu_custom_call", output_to_operand_aliasing={{}: (4, {})} | custom-call | flops 21474836480 | bytes 25165824 | tf_op jit(solution)/shard_map/forward_at_8/pallas_call | solution.py:174
  583.0 0.0 copy-start.1
  583.0 111.9 %focus.1 = f32[2,256,16384]{2,1,0:T(8,128)} custom-call(s32[16,8]{1,0:T(8,128)} %copy.19.shift_ref, f32[16,8]{1,0:T(8,128)} %fusion.3.weight_ref, bf16[2,256,256]{2,1,0:T(8,128)(2,1)} %constant.74.table_ref, f32[128,128]{1,0:T(8,128)} %constant.60.clone.cos_ref, f32[128,128]{1,0:T(8,128)} %constant.61.clone.sin_ref, ...), custom_call_target="tpu_custom_call" | custom-call | tf_op jit(solution)/shard_map/focus/pallas_call | solution.py:262
  694.9 0.0 copy-done.1
  (7 shorter events, 0.2 us)
Async XLA Ops:
  0.0 403.0 %copy-start = (f32[512,8]{0,1:T(8,128)S(1)}, f32[512,8]{0,1:T(8,128)}, u32[]{:S(2)}) copy-start(f32[512,8]{0,1:T(8,128)} %param.16) | copy-start | bytes 49156
  0.0 183.2 %collective-permute-start = (bf16[2,2048,2048]{2,1,0:T(8,128)(2,1)}, bf16[2,2048,2048]{2,1,0:T(8,128)(2,1)}, u32[]{:S(2)}, u32[]{:S(2)}) collective-permute-start(bf16[2,2048,2048]{2,1,0:T(8,128)(2,1)} %own_ref.3), channel_id=1, source_target_pairs={{1,0},{2,1},{3,2},{5,4},{6,5},{7,6},{9,8},{10,9},{11,10},{13,12},{... | collective-permute-start | bytes 50331656 | tf_op jit(solution)/shard_map/ppermute | solution.py:301
  242.2 130.9 %all-to-all-start.1 = ((bf16[8,2,128,2048]{3,2,1,0:T(8,128)(2,1)}), bf16[8,2,128,2048]{3,2,1,0:T(8,128)(2,1)}, u32[]{:S(2)}, u32[]{:S(2)}) async-start(bf16[8,2,128,2048]{3,2,1,0:T(8,128)(2,1)} %compress_0.1), calls=%async_computation.1 | async-start | bytes 16777216 | tf_op jit(solution)/shard_map/all_to_all | solution.py:332
  373.2 170.9 %all-to-all-start = ((bf16[8,2,128,2048]{3,2,1,0:T(8,128)(2,1)}), bf16[8,2,128,2048]{3,2,1,0:T(8,128)(2,1)}, u32[]{:S(2)}, u32[]{:S(2)}) async-start(bf16[8,2,128,2048]{3,2,1,0:T(8,128)(2,1)} %compress_1.1), calls=%async_computation | async-start | bytes 16777216 | tf_op jit(solution)/shard_map/all_to_all | solution.py:332
  412.6 92.3 %collective-permute-start.1 = (bf16[8,2,32,2048]{3,2,1,0:T(8,128)(2,1)}, bf16[8,2,32,2048]{3,2,1,0:T(8,128)(2,1)S(1)}, u32[]{:S(2)}, u32[]{:S(2)}) collective-permute-start(bf16[8,2,32,2048]{3,2,1,0:T(8,128)(2,1)} %slice.22), channel_id=1, source_target_pairs={{4,0},{8,4},{12,8},{16,12},{20,16},{24,20},{28,24},{1,28},{5,1},{9... | collective-permute-start | bytes 6291464 | tf_op jit(solution)/shard_map/ppermute | solution.py:336
  504.9 1.3 copy-start.2
  583.0 111.9 %copy-start.1 = (f32[512,8]{0,1:T(8,128)S(1)}, f32[512,8]{0,1:T(8,128)}, u32[]{:S(2)}) copy-start(f32[512,8]{0,1:T(8,128)} %param.16) | copy-start | bytes 49156
